TPU v7x, 32 devices: a whole 2x2x4 slice. The times are simulated.
32 devices in a mesh: row: 4 (over y, core), col: 8 (over z, x).
Axes of the slice: x: 2, y: 2, z: 4, core: 2. Of those that a mesh axis runs over, the one named last changes fastest.
Arguments:
- noise: bfloat16 [4096, 4096], P('row', 'col'), may hold values from -6 to 6
- latents: bfloat16 [8192, 4096], P('col', 'row'), may hold values from -12 to 12
Outputs:
- transported: bfloat16 [4096, 4096], P('row', 'col')
- row_potential: float32 [4096], P('row')
- col_potential: float32 [8192], P('col')
All inputs are finite; a program needn't handle non-finite values.
Results may differ from a plain program's by a relative error of at most 0.018.
Values may be sent and summed in bfloat16 or wider, within the bound.
A program may use at most 64 MiB of HBM per device.

v0:
```python
import math

import jax
import jax.numpy as jnp
from jax import lax
from jax.sharding import PartitionSpec as P

ITERS = 3


epsilon = 0.01


def row_logsum(scores):
    high = lax.pmax(jnp.max(scores, axis=1), "col")
    total = lax.psum(jnp.sum(jnp.exp(scores - high[:, None]), axis=1), "col")
    return high + jnp.log(total)


def col_logsum(scores):
    high = lax.pmax(jnp.max(scores, axis=0), "row")
    total = lax.psum(jnp.sum(jnp.exp(scores - high[None, :]), axis=0), "row")
    return high + jnp.log(total)


def on_device(noise, latents):
    local_rows = noise.shape[0]
    whole_lat = lax.all_gather(latents, "row", axis=1, tiled=True)
    local_cols = whole_lat.shape[0]
    width = whole_lat.shape[1]
    cross = lax.dot_general(
        lax.all_gather(noise, "col", axis=1, tiled=True),
        whole_lat,
        (((1,), (1,)), ((), ())),
        preferred_element_type=jnp.float32,
    )
    logits = cross * (2.0 / (width * epsilon))
    noise_count = local_rows * lax.axis_size("row")
    latent_count = local_cols * lax.axis_size("col")
    col_potential = jnp.zeros((local_cols,), jnp.float32)
    row_potential = jnp.zeros((local_rows,), jnp.float32)
    for step in range(ITERS):
        row_potential = -math.log(noise_count) - row_logsum(logits + col_potential[None, :])
        col_potential = -math.log(latent_count) - col_logsum(logits + row_potential[:, None])
    plan = jnp.exp(logits + row_potential[:, None] + col_potential[None, :]).astype(jnp.bfloat16)
    mass = lax.psum(jnp.sum(plan.astype(jnp.float32), axis=1), "col")
    numerator = jnp.dot(plan, whole_lat, preferred_element_type=jnp.float32)
    shares = lax.psum_scatter(
        numerator.astype(jnp.bfloat16), "col", scatter_dimension=1, tiled=True
    ).astype(jnp.float32)
    transported = (shares / mass[:, None]).astype(jnp.bfloat16)
    return (transported, row_potential, col_potential)


def solution(mesh):
    in_specs = (P("row", "col"), P("col", "row"))
    out_specs = (P("row", "col"), P("row"), P("col"))
    return jax.shard_map(
        on_device, mesh=mesh, in_specs=in_specs, out_specs=out_specs, check_vma=False
    )
```

profile of v0, /device:TPU:9, one launch (start us, length us, event | category | flops | bytes accessed | tf_op | source)
XLA Modules:
  0.0 556.5 jit_solution(8138596448945822952)
XLA Ops:
  7.2 0.0 all-gather.5.cloned.1.call-start
  7.2 0.7 all-gather.5.cloned.1.call-update
  7.9 0.0 all-gather.3.cloned.1.call-start
  7.9 0.7 all-gather.3.cloned.1.call-update
  8.6 0.0 reduce-scatter.2.cloned.1.call-start
  8.7 60.8 %all-gather.5.cloned.1.call-done = bf16[1024,4096]{1,0:T(8,128)(2,1)} async-done(((bf16[1024,1024]{1,0:T(8,128)(2,1)}), bf16[1024,4096]{1,0:T(8,128)(2,1)}) %all-gather.5.cloned.1.call-update) | async-done | bytes 8388624 | tf_op jit(solution)/shard_map/all_gather | solution.py:28
  69.5 124.8 %all-gather.3.cloned.1.call-done = bf16[1024,4096]{1,0:T(8,128)(2,1)} async-done(((bf16[1024,512]{1,0:T(8,128)(2,1)}), bf16[1024,4096]{1,0:T(8,128)(2,1)}) %all-gather.3.cloned.1.call-update) | async-done | bytes 8388624 | tf_op jit(solution)/shard_map/all_gather | solution.py:32
  194.3 15.0 %fusion = (f32[1024]{0:T(1024)S(1)}, f32[1024,1024]{0,1:T(8,128)}) fusion(bf16[1024,4096]{1,0:T(8,128)(2,1)} %all-gather.3.cloned.1.call-done, bf16[1024,4096]{1,0:T(8,128)(2,1)} %all-gather.5.cloned.1.call-done), kind=kOutput, calls=%fused_computation.22 | convolution fusion | flops 8592030720 | bytes 20975616 | tf_op jit(solution)/shard_map/dot_general | solution.py:31
  209.3 14.6 %pmax.42 = f32[1024]{0:T(1024)S(1)} all-reduce(f32[1024]{0:T(1024)S(1)} %get-tuple-element.3), channel_id=1, replica_groups=mesh['row'=4,'col'=8] {'col'}, use_global_device_ids=true, to_apply=%region_1.0 | all-reduce | flops 1024 | bytes 8192 | tf_op jit(solution)/shard_map/pmax | solution.py:15
  223.9 2.8 exponential_reduce_fusion.5
  226.7 13.7 %psum.49 = f32[1024]{0:T(1024)S(1)} all-reduce(f32[1024]{0:T(1024)S(1)} %exponential_reduce_fusion.5), channel_id=1, replica_groups=mesh['row'=4,'col'=8] {'col'}, use_global_device_ids=true, to_apply=%region_3.0 | all-reduce | flops 1024 | bytes 8192 | tf_op jit(solution)/shard_map/psum | solution.py:16
  240.3 2.5 add_reduce_fusion.3
  242.9 13.2 %pmax.43 = f32[1024]{0:T(1024)S(1)} all-reduce(f32[1024]{0:T(1024)S(1)} %add_reduce_fusion.3), channel_id=1, replica_groups=mesh['row'=4,'col'=8] {'row'}, use_global_device_ids=true, to_apply=%region_5.0 | all-reduce | flops 1024 | bytes 8192 | tf_op jit(solution)/shard_map/pmax | solution.py:21
  256.1 3.1 exponential_reduce_fusion.4
  259.2 5.8 %psum.50 = f32[1024]{0:T(1024)S(1)} all-reduce(f32[1024]{0:T(1024)S(1)} %exponential_reduce_fusion.4), channel_id=1, replica_groups=mesh['row'=4,'col'=8] {'row'}, use_global_device_ids=true, to_apply=%region_7.0 | all-reduce | flops 1024 | bytes 8192 | tf_op jit(solution)/shard_map/psum | solution.py:22
  265.0 2.5 add_reduce_fusion.2
  267.5 14.9 %pmax.44 = f32[1024]{0:T(1024)S(1)} all-reduce(f32[1024]{0:T(1024)S(1)} %add_reduce_fusion.2), channel_id=1, replica_groups=mesh['row'=4,'col'=8] {'col'}, use_global_device_ids=true, to_apply=%region_9.0 | all-reduce | flops 1024 | bytes 8192 | tf_op jit(solution)/shard_map/pmax | solution.py:15
  282.4 2.9 exponential_reduce_fusion.3
  285.4 14.2 %psum.51 = f32[1024]{0:T(1024)S(1)} all-reduce(f32[1024]{0:T(1024)S(1)} %exponential_reduce_fusion.3), channel_id=1, replica_groups=mesh['row'=4,'col'=8] {'col'}, use_global_device_ids=true, to_apply=%region_11.0 | all-reduce | flops 1024 | bytes 8192 | tf_op jit(solution)/shard_map/psum | solution.py:16
  299.5 2.5 add_reduce_fusion.1
  302.1 13.7 %pmax.45 = f32[1024]{0:T(1024)S(1)} all-reduce(f32[1024]{0:T(1024)S(1)} %add_reduce_fusion.1), channel_id=1, replica_groups=mesh['row'=4,'col'=8] {'row'}, use_global_device_ids=true, to_apply=%region_13.0 | all-reduce | flops 1024 | bytes 8192 | tf_op jit(solution)/shard_map/pmax | solution.py:21
  315.8 3.1 exponential_reduce_fusion.2
  318.9 5.7 %psum.52 = f32[1024]{0:T(1024)S(1)} all-reduce(f32[1024]{0:T(1024)S(1)} %exponential_reduce_fusion.2), channel_id=1, replica_groups=mesh['row'=4,'col'=8] {'row'}, use_global_device_ids=true, to_apply=%region_15.0 | all-reduce | flops 1024 | bytes 8192 | tf_op jit(solution)/shard_map/psum | solution.py:22
  324.6 2.5 add_reduce_fusion
  327.1 14.8 %pmax.46 = f32[1024]{0:T(1024)S(1)} all-reduce(f32[1024]{0:T(1024)S(1)} %add_reduce_fusion), channel_id=1, replica_groups=mesh['row'=4,'col'=8] {'col'}, use_global_device_ids=true, to_apply=%region_17.0 | all-reduce | flops 1024 | bytes 8192 | tf_op jit(solution)/shard_map/pmax | solution.py:15
  341.9 2.9 exponential_reduce_fusion.1
  344.9 14.2 %psum.53 = f32[1024]{0:T(1024)S(1)} all-reduce(f32[1024]{0:T(1024)S(1)} %exponential_reduce_fusion.1), channel_id=1, replica_groups=mesh['row'=4,'col'=8] {'col'}, use_global_device_ids=true, to_apply=%region_19.0 | all-reduce | flops 1024 | bytes 8192 | tf_op jit(solution)/shard_map/psum | solution.py:16
  359.1 0.0 copy-start
  359.1 2.5 add_reduce_fusion.4
  361.7 13.5 %pmax.47 = f32[1024]{0:T(1024)S(1)} all-reduce(f32[1024]{0:T(1024)S(1)} %add_reduce_fusion.4), channel_id=1, replica_groups=mesh['row'=4,'col'=8] {'row'}, use_global_device_ids=true, to_apply=%region_21.0 | all-reduce | flops 1024 | bytes 8192 | tf_op jit(solution)/shard_map/pmax | solution.py:21
  375.2 3.1 exponential_reduce_fusion
  378.2 5.7 %psum.54 = f32[1024]{0:T(1024)S(1)} all-reduce(f32[1024]{0:T(1024)S(1)} %exponential_reduce_fusion), channel_id=1, replica_groups=mesh['row'=4,'col'=8] {'row'}, use_global_device_ids=true, to_apply=%region_23.0 | all-reduce | flops 1024 | bytes 8192 | tf_op jit(solution)/shard_map/psum | solution.py:22
  383.9 0.0 copy-start.1
  383.9 15.0 %convolution_convert_fusion = bf16[1024,4096]{1,0:T(8,128)(2,1)} fusion(bf16[1024,4096]{1,0:T(8,128)(2,1)} %all-gather.5.cloned.1.call-done, f32[1024,1024]{0,1:T(8,128)} %get-tuple-element.4, f32[1024]{0:T(1024)S(1)} %add_subtract_fusion, f32[1024]{0:T(1024)S(1)} %add_subtract_fusion.1), kind=kOutput, calls=%fused_computation | convolution fusion | flops 8597274624 | bytes 20979712 | tf_op jit(solution)/shard_map/dot_general | solution.py:47
  398.9 0.0 reduce-scatter.2.cloned.1.call-update
  398.9 0.0 copy-done
  398.9 0.0 copy-done.1
  398.9 2.9 convert_reduce_fusion
  401.9 15.8 %psum.55 = f32[1024]{0:T(1024)S(1)} all-reduce(f32[1024]{0:T(1024)S(1)} %convert_reduce_fusion), channel_id=1, replica_groups=mesh['row'=4,'col'=8] {'col'}, use_global_device_ids=true, to_apply=%region_26.0 | all-reduce | flops 1024 | bytes 8192 | tf_op jit(solution)/shard_map/psum | solution.py:46
  417.7 129.8 %reduce-scatter.2.cloned.1.call-done = bf16[1024,512]{1,0:T(8,128)(2,1)} async-done(((bf16[1024,4096]{1,0:T(8,128)(2,1)}), bf16[1024,512]{1,0:T(8,128)(2,1)}) %reduce-scatter.2.cloned.1.call-update) | async-done | bytes 1048592 | tf_op jit(solution)/shard_map/reduce_scatter | solution.py:48
  547.5 2.5 divide_convert_fusion
  (6 shorter events, 0.1 us)
Async XLA Ops:
  7.2 62.3 %all-gather.5.cloned.1.call-start = ((), (), s32[]{:S(2)}) async-start(), calls=%async_computation.2 | async-start | bytes 10485760 | tf_op jit(solution)/shard_map/all_gather | solution.py:28
  7.9 186.4 %all-gather.3.cloned.1.call-start = ((), (), s32[]{:S(2)}) async-start(), calls=%async_computation.1 | async-start | bytes 9437184 | tf_op jit(solution)/shard_map/all_gather | solution.py:32
  8.6 538.9 %reduce-scatter.2.cloned.1.call-start = ((), (), s32[]{:S(2)}) async-start(), calls=%async_computation.3 | async-start | bytes 9437184 | tf_op jit(solution)/shard_map/reduce_scatter | solution.py:48
  359.1 39.8 %copy-start = (f32[1024]{0:T(1024)}, f32[1024]{0:T(1024)S(1)}, u32[]{:S(2)}) copy-start(f32[1024]{0:T(1024)S(1)} %add_subtract_fusion.1) | copy-start | bytes 12292
  383.9 15.0 %copy-start.1 = (f32[1024]{0:T(1024)}, f32[1024]{0:T(1024)S(1)}, u32[]{:S(2)}) copy-start(f32[1024]{0:T(1024)S(1)} %add_subtract_fusion) | copy-start | bytes 12292
Sparse Core Ops, SparseCore 0:
  9.6 59.8 all-gather.4
  71.5 122.7 all-gather.2
  399.0 148.4 reduce-scatter.1
where the time goes:
time: 560 us; the launch traced here: 557 us
  waiting for transfers between devices  317 us (57%)
  blocking collectives  160 us (29%)
  other arithmetic  36 us (6%)
  matrix products  30 us (5%)
  between operations  13.8 us (2%)
    reduce_scatter x1, waiting for transfers between devices, on_device(): lax.psum_scatter(numerator.astype(jnp.bfloat16), 'col', scatter_dimension...  130 us
    all_gather x1, waiting for transfers between devices, on_device(): lax.all_gather(noise, 'col', axis=1, tiled=True)  125 us
    all_gather x1, waiting for transfers between devices, on_device(): whole_lat = lax.all_gather(latents, 'row', axis=1, tiled=True)  60.8 us
    pmax x3, blocking collectives, row_logsum(): high = lax.pmax(jnp.max(scores, axis=1), 'col')  44.3 us
    psum x3, blocking collectives, row_logsum(): total = lax.psum(jnp.sum(jnp.exp(scores - high[:, None]), axis=1), 'col')  42.1 us
    pmax x3, blocking collectives, col_logsum(): high = lax.pmax(jnp.max(scores, axis=0), 'row')  40.4 us
    psum x3, blocking collectives, col_logsum(): total = lax.psum(jnp.sum(jnp.exp(scores - high[None, :]), axis=0), 'row')  17.1 us
    psum x1, blocking collectives, on_device(): mass = lax.psum(jnp.sum(plan.astype(jnp.float32), axis=1), 'col')  15.8 us
  transfers between devices with their start and end apart: 3, of which 3 were waited for; matrix products, arithmetic and copies ran while one was open for 1% of the time, Pallas kernels for 0%

commit v1 on v0

v1 whole, which is shorter than its diff:
```python
import functools
import math

import jax
import jax.numpy as jnp
from jax import lax
from jax.experimental import pallas as pl
from jax.experimental.pallas import tpu as pltpu
from jax.sharding import PartitionSpec as P

ITERS = 3
EPSILON = 0.01
LANES = 128
MESH = pl.DeviceIdType.MESH


def kernel(
    nr, nc, noise, lat,
    out, row_out, col_out,
    noise_all, lat_all, logits, plan, rowb, mt, st, mc, sc, colp,
    row_box, col_box, x_send, x_recv, own, z_low, z_high, num,
    local_sem, ng_send, ng_recv, lg_send, lg_recv,
    row_send, row_recv, col_send, col_recv,
    xs_sem, xr_sem, up_sem, low_sem, down_sem, high_sem,
):
    rows, kn = noise.shape
    cols, kl = lat.shape
    width = kl * nr
    hi = nc // 2
    groups = cols // LANES
    scale = 2.0 / (width * EPSILON)
    r = lax.axis_index("row")
    c = lax.axis_index("col")
    h, l = lax.div(c, 2), lax.rem(c, 2)
    rh, rl = lax.div(r, 2), lax.rem(r, 2)

    barrier = pltpu.get_barrier_semaphore()
    for d in range(1, nc):
        pl.semaphore_signal(barrier, inc=1, device_id={"col": lax.rem(c + d, nc)}, device_id_type=MESH)
    for d in range(1, nr):
        pl.semaphore_signal(barrier, inc=1, device_id={"row": lax.rem(r + d, nr)}, device_id_type=MESH)
    pl.semaphore_wait(barrier, nc - 1 + nr - 1)

    def noise_slot(j):
        return noise_all.at[lax.div(j, 2), :, pl.ds(pl.multiple_of(lax.rem(j, 2) * kn, kn), kn)]

    def lat_slot(j):
        return lat_all.at[j]

    def remote(src, dst, send, recv, axis, target):
        return pltpu.make_async_remote_copy(
            src_ref=src, dst_ref=dst, send_sem=send, recv_sem=recv,
            device_id={axis: target}, device_id_type=MESH,
        )

    class Gather:
        def __init__(self, axis, n, own_ref, slot, send, recv, ah, al):
            self.axis, self.half, self.own, self.slot = axis, n // 2, own_ref, slot
            self.send, self.recv, self.h, self.l = send, recv, ah, al
            self.me = 2 * ah + al

        def copy(self, kind, j, src):
            target = (self.me + 1 - 2 * self.l, self.me + 2, self.me - 2)[kind]
            return remote(
                src, self.slot(j), self.send.at[kind, lax.div(j, 2)], self.recv.at[j], self.axis, target
            )

        def first(self):
            @pl.when(self.h < self.half - 1)
            def _():
                self.copy(1, self.me, self.own).start()

            @pl.when(self.h > 0)
            def _():
                self.copy(2, self.me, self.own).start()

            self.copy(0, self.me, self.own).start()

        def arrived(self, j):
            self.copy(0, j, self.slot(j)).wait_recv()

        def forward(self, s):
            @pl.when(self.h - s >= 0)
            def _():
                j = self.me - 2 * s
                self.arrived(j)

                @pl.when(self.h < self.half - 1)
                def _():
                    self.copy(1, j, self.slot(j)).start()

                self.copy(0, j, self.slot(j)).start()

            @pl.when(self.h + s < self.half)
            def _():
                j = self.me + 2 * s
                self.arrived(j)

                @pl.when(self.h > 0)
                def _():
                    self.copy(2, j, self.slot(j)).start()

                self.copy(0, j, self.slot(j)).start()

        def other(self, k):
            self.arrived(2 * k + 1 - self.l)

        def finish(self):
            @pl.loop(0, self.half)
            def _(k):
                j = 2 * k + self.l
                self.copy(0, j, self.slot(j)).wait_send()

                @pl.when((k <= self.h) & (self.h < self.half - 1))
                def _():
                    self.copy(1, j, self.slot(j)).wait_send()

                @pl.when((k >= self.h) & (self.h > 0))
                def _():
                    self.copy(2, j, self.slot(j)).wait_send()

    noise_g = Gather("col", nc, noise, noise_slot, ng_send, ng_recv, h, l)
    lat_g = Gather("row", nr, lat, lat_slot, lg_send, lg_recv, rh, rl)
    noise_g.first()
    lat_g.first()
    mine = [
        pltpu.make_async_copy(noise, noise_slot(c), local_sem.at[0]),
        pltpu.make_async_copy(lat, lat_slot(r), local_sem.at[1]),
    ]
    for copy in mine:
        copy.start()
    colp[...] = jnp.zeros_like(colp)

    tile_n = min(256, cols)

    def block(k, add):
        @pl.loop(0, cols // tile_n)
        def _(t):
            span = pl.ds(pl.multiple_of(t * tile_n, tile_n), tile_n)
            part = lax.dot_general(
                noise_all[k], lat_all[k, span, :], (((1,), (1,)), ((), ())),
                preferred_element_type=jnp.float32,
            ) * scale
            if add:
                logits[:, span] += part
            else:
                logits[:, span] = part

    def blocks(s):
        @pl.loop(0, 2)
        def _(side):
            k = h + s * (2 * side - 1)

            @pl.when((k >= 0) & (k < hi))
            def _():
                noise_g.other(k)
                block(k, True)

    for s in range(1, min(3, hi)):
        noise_g.forward(s)
    for s in range(1, nr // 2):
        lat_g.forward(s)
    for copy in mine:
        copy.wait()

    @pl.loop(0, nr // 2)
    def _(k):
        lat_g.other(k)

    noise_g.other(h)
    block(h, False)
    if hi > 1:
        blocks(1)
    for s in range(3, hi):
        noise_g.forward(s)
        blocks(s - 1)
    if hi > 2:
        blocks(hi - 1)

    def exchange(axis, n, me, box, send, recv):
        for d in range(1, n):
            remote(box.at[me], box.at[me], send.at[d], recv.at[me], axis, lax.rem(me + d, n)).start()
        for d in range(1, n):
            j = lax.rem(me + n - d, n)
            remote(box.at[j], box.at[j], send.at[d], recv.at[j], axis, j).wait_recv()

    def sent(axis, n, me, box, send, recv):
        for d in range(1, n):
            remote(box.at[me], box.at[me], send.at[d], recv.at[me], axis, lax.rem(me + d, n)).wait_send()

    def merged(n, box):
        high = functools.reduce(jnp.maximum, [box[j, 0:1, :] for j in range(n)])
        total = functools.reduce(
            jnp.add, [box[j, 1:2, :] * jnp.exp(box[j, 0:1, :] - high) for j in range(n)]
        )
        return high + jnp.log(total)

    def lane(g):
        return pl.ds(g * LANES, LANES)

    row_tile = 32
    col_tile = 64

    for step in range(ITERS):
        @pl.loop(0, rows // row_tile, unroll=2)
        def _(t):
            span = pl.ds(pl.multiple_of(t * row_tile, row_tile), row_tile)
            v = [logits[span, lane(g)] + colp[:, lane(g)] for g in range(groups)]
            m = functools.reduce(jnp.maximum, v)
            mt[span, :] = m
            st[span, :] = functools.reduce(jnp.add, [jnp.exp(x - m) for x in v])

        m = mt[...].T
        high = jnp.max(m, axis=0, keepdims=True)
        box = row_box.at[step]
        mine_box = box.at[c]
        mine_box[0:1, :] = high
        mine_box[1:2, :] = jnp.sum(st[...].T * jnp.exp(m - high), axis=0, keepdims=True)
        exchange("col", nc, c, box, row_send.at[step], row_recv.at[step])
        rowp = -math.log(rows * nr) - merged(nc, box)
        row_out[...] = rowp
        rowb[...] = jnp.broadcast_to(rowp, (LANES, rows)).T

        @pl.loop(0, rows // col_tile)
        def _(t):
            span = pl.ds(pl.multiple_of(t * col_tile, col_tile), col_tile)
            small = pl.ds(pl.multiple_of(t * 8, 8), 8)
            shift = rowb[span, :]
            for g in range(groups):
                v = (logits[span, lane(g)] + shift).reshape(col_tile // 8, 8, LANES)
                m = jnp.max(v, axis=0)
                mc[small, lane(g)] = m
                sc[small, lane(g)] = jnp.sum(jnp.exp(v - m[None]), axis=0)

        m = mc[...]
        high = jnp.max(m, axis=0, keepdims=True)
        box = col_box.at[step]
        mine_box = box.at[r]
        mine_box[0:1, :] = high
        mine_box[1:2, :] = jnp.sum(sc[...] * jnp.exp(m - high), axis=0, keepdims=True)
        exchange("row", nr, r, box, col_send.at[step], col_recv.at[step])
        colp[...] = -math.log(cols * nc) - merged(nr, box)
    col_out[...] = colp[...]

    @pl.loop(0, rows // row_tile, unroll=2)
    def _(t):
        span = pl.ds(pl.multiple_of(t * row_tile, row_tile), row_tile)
        shift = rowb[span, :]
        total = jnp.zeros((row_tile, LANES), jnp.float32)
        for g in range(groups):
            p = jnp.exp(logits[span, lane(g)] + shift + colp[:, lane(g)]).astype(jnp.bfloat16)
            plan[span, lane(g)] = p
            total += p.astype(jnp.float32)
        mt[span, :] = total

    tile_k = min(256, kn)

    def share(k, side, dst):
        @pl.loop(0, kn // tile_k)
        def _(t):
            off = pl.multiple_of(t * tile_k, tile_k)
            src = pl.multiple_of(side * kn + t * tile_k, tile_k)
            dst[:, pl.ds(off, tile_k)] = jnp.dot(
                plan[...], lat_all[k, :, pl.ds(src, tile_k)], preferred_element_type=jnp.float32
            ).astype(jnp.bfloat16)

    partner = c + 1 - 2 * l

    def x_copy(k):
        return remote(x_send.at[k], x_recv.at[k], xs_sem.at[k], xr_sem.at[k], "col", partner)

    def up_copy(k):
        return remote(own.at[k], z_low.at[k], up_sem.at[k], low_sem.at[k], "col", c + 2)

    def down_copy(k):
        return remote(own.at[k], z_high.at[k], down_sem.at[k], high_sem.at[k], "col", c - 2)

    def farthest_first(body):
        @pl.loop(0, 2 * hi - 1)
        def _(p):
            s = hi - 1 - lax.div(p, 2)
            k = h + s * (1 - 2 * lax.rem(p, 2))

            @pl.when((k >= 0) & (k < hi))
            def _():
                body(k)

    def send_share(k):
        share(k, 1 - l, x_send.at[k])
        x_copy(k).start()

    farthest_first(send_share)

    mine_box = row_box.at[ITERS, c]
    mine_box[0:1, :] = jnp.sum(mt[...].T, axis=0, keepdims=True)
    mine_box[1:2, :] = jnp.zeros((1, rows), jnp.float32)
    exchange("col", nc, c, row_box.at[ITERS], row_send.at[ITERS], row_recv.at[ITERS])
    mass = functools.reduce(jnp.add, [row_box[ITERS, j, 0:1, :] for j in range(nc)])
    rowb[...] = jnp.broadcast_to(1.0 / mass, (LANES, rows)).T

    farthest_first(lambda k: share(k, l, own.at[k]))

    f32 = jnp.float32
    add_tile = min(128, rows)

    def tiles(body):
        @pl.loop(0, rows // add_tile)
        def _(t):
            body(pl.ds(pl.multiple_of(t * add_tile, add_tile), add_tile))

    def add_two(k):
        def body(span):
            own[k, span, :] = (own[k, span, :].astype(f32) + x_recv[k, span, :].astype(f32)).astype(jnp.bfloat16)
        tiles(body)

    def add_three(k, third):
        def body(span):
            own[k, span, :] = (
                own[k, span, :].astype(f32) + x_recv[k, span, :].astype(f32) + third[k, span, :].astype(f32)
            ).astype(jnp.bfloat16)
        tiles(body)

    def relay(k):
        x_copy(k).wait_recv()

        @pl.when(k > h)
        def _():
            @pl.when(h > 0)
            def _():
                up_copy(k).wait_recv()
                add_three(k, z_low)

            @pl.when(h == 0)
            def _():
                add_two(k)

            up_copy(k).start()

        @pl.when(k < h)
        def _():
            @pl.when(h < hi - 1)
            def _():
                down_copy(k).wait_recv()
                add_three(k, z_high)

            @pl.when(h == hi - 1)
            def _():
                add_two(k)

            down_copy(k).start()

    farthest_first(relay)

    def start_sum(span):
        num[span, :] = own[h, span, :].astype(f32) + x_recv[h, span, :].astype(f32)

    tiles(start_sum)

    @pl.when(h > 0)
    def _():
        up_copy(h).wait_recv()

        def body(span):
            num[span, :] += z_low[h, span, :].astype(f32)
        tiles(body)

    @pl.when(h < hi - 1)
    def _():
        down_copy(h).wait_recv()

        def body(span):
            num[span, :] += z_high[h, span, :].astype(f32)
        tiles(body)

    def last(span):
        inverse = rowb[span, :]
        for g in range(kn // LANES):
            out[span, lane(g)] = (num[span, lane(g)] * inverse).astype(jnp.bfloat16)

    tiles(last)

    noise_g.finish()
    lat_g.finish()
    for step in range(ITERS + 1):
        sent("col", nc, c, row_box.at[step], row_send.at[step], row_recv.at[step])
    for step in range(ITERS):
        sent("row", nr, r, col_box.at[step], col_send.at[step], col_recv.at[step])

    @pl.loop(0, hi)
    def _(k):
        x_copy(k).wait_send()

        @pl.when(k > h)
        def _():
            up_copy(k).wait_send()

        @pl.when(k < h)
        def _():
            down_copy(k).wait_send()


def on_device(nr, nc, noise, latents):
    rows, kn = noise.shape
    cols, kl = latents.shape
    hi = nc // 2
    bf16, f32 = jnp.bfloat16, jnp.float32
    vmem, dma = pltpu.VMEM, pltpu.SemaphoreType.DMA
    transported, row_potential, col_potential = pl.pallas_call(
        functools.partial(kernel, nr, nc),
        out_shape=(
            jax.ShapeDtypeStruct((rows, kn), bf16),
            jax.ShapeDtypeStruct((1, rows), f32),
            jax.ShapeDtypeStruct((1, cols), f32),
        ),
        in_specs=[pl.BlockSpec(memory_space=pl.ANY)] * 2,
        out_specs=[pl.BlockSpec(memory_space=pltpu.VMEM)] * 3,
        scratch_shapes=[
            vmem((hi, rows, 2 * kn), bf16),
            vmem((nr, cols, kl), bf16),
            vmem((rows, cols), f32),
            vmem((rows, cols), bf16),
            vmem((rows, LANES), f32),
            vmem((rows, LANES), f32),
            vmem((rows, LANES), f32),
            vmem((rows // 8, cols), f32),
            vmem((rows // 8, cols), f32),
            vmem((1, cols), f32),
            vmem((ITERS + 1, nc, 2, rows), f32),
            vmem((ITERS, nr, 2, cols), f32),
            vmem((hi, rows, kn), bf16),
            vmem((hi, rows, kn), bf16),
            vmem((hi, rows, kn), bf16),
            vmem((hi, rows, kn), bf16),
            vmem((hi, rows, kn), bf16),
            vmem((rows, kn), f32),
            dma((2,)),
            dma((3, hi)), dma((nc,)),
            dma((3, nr // 2)), dma((nr,)),
            dma((ITERS + 1, nc)), dma((ITERS + 1, nc)),
            dma((ITERS, nr)), dma((ITERS, nr)),
            dma((hi,)), dma((hi,)), dma((hi,)), dma((hi,)), dma((hi,)), dma((hi,)),
        ],
        compiler_params=pltpu.CompilerParams(
            collective_id=0, has_side_effects=True, vmem_limit_bytes=58 * 2**20
        ),
        cost_estimate=pl.CostEstimate(
            flops=4 * rows * cols * kl * nr, bytes_accessed=8 * 2**20, transcendentals=7 * rows * cols
        ),
    )(noise, latents)
    return transported, row_potential.reshape(rows), col_potential.reshape(cols)


def solution(mesh):
    in_specs = (P("row", "col"), P("col", "row"))
    out_specs = (P("row", "col"), P("row"), P("col"))
    return jax.shard_map(
        functools.partial(on_device, mesh.shape["row"], mesh.shape["col"]),
        mesh=mesh, in_specs=in_specs, out_specs=out_specs, check_vma=False,
    )
```

time: 560 us -> 310 us (0.55)
  waiting for transfers between devices: 317 us -> 0 us
  Pallas kernels: 0 us -> 301 us
  blocking collectives: 160 us -> 0 us
  other arithmetic: 36 us -> 0 us
  matrix products: 30 us -> 0 us
  between operations: 13.8 us -> 0.66 us
    pallas_call x0 -> x1, Pallas kernels: none -> 301 us  [on_device(): pl.pallas_call(functools.partial(kernel, nr, nc), out_shape=(jax.ShapeDty...]
    all_gather x2 -> x0, waiting for transfers between devices: 186 us -> none  [the longest x1 125 us: on_device(): lax.all_gather(noise, 'col', axis=1, tiled=True)]
    reduce_scatter x1 -> x0, waiting for transfers between devices: 130 us -> none  [on_device(): lax.psum_scatter(numerator.astype(jnp.bfloat16), 'col', scatter_dimension...]
    pmax x6 -> x0, blocking collectives: 84.8 us -> none  [the longest x3 44.3 us: row_logsum(): high = lax.pmax(jnp.max(scores, axis=1), 'col')]
    psum x7 -> x0, blocking collectives: 75 us -> none  [the longest x3 42.1 us: row_logsum(): total = lax.psum(jnp.sum(jnp.exp(scores - high[:, None]), axis=1), 'col')]
    dot_general x2 -> x0, matrix products: 30 us -> none  [the longest x1 15 us: on_device(): lax.dot_general(lax.all_gather(noise, 'col', axis=1, tiled=True), whole_l...]
    reduce_sum x7 -> x0, other arithmetic: 20.8 us -> none  [the longest x3 9.19 us: col_logsum(): total = lax.psum(jnp.sum(jnp.exp(scores - high[None, :]), axis=0), 'row')]
    reduce_max x5 -> x0, other arithmetic: 12.7 us -> none  [the longest x3 7.62 us: col_logsum(): high = lax.pmax(jnp.max(scores, axis=0), 'row')]
  transfers between devices with their start and end apart: 3 -> 0, of which waited for: 3 -> 0; matrix products, arithmetic and copies ran while one was open for 1% -> 0% of each run, Pallas kernels for 0% -> 0%
where the time goes in v1:
time: 310 us; the launch traced here: 305 us
  Pallas kernels  301 us (97%)
  local copies, waits for them, and re-layouts  3.46 us (1%)
    pallas_call x1, Pallas kernels, on_device(): pl.pallas_call(functools.partial(kernel, nr, nc), out_shape=(jax.ShapeDty...  301 us

profile of v1, /device:TPU:9, one launch (start us, length us, event | category | flops | bytes accessed | tf_op | source)
XLA Modules:
  0.0 305.3 jit_solution(6667327991256675058)
XLA Ops:
  0.6 301.1 %shard_map.49 = (bf16[1024,512]{1,0:T(8,128)(2,1)}, f32[1,1024]{1,0:T(1,128)}, f32[1,1024]{1,0:T(1,128)}) custom-call(bf16[1024,512]{1,0:T(8,128)(2,1)} %noise.1, bf16[1024,1024]{1,0:T(8,128)(2,1)} %lat.1), custom_call_target="tpu_custom_call" | custom-call | flops 17179869184 | bytes 8388608 | tf_op jit(solution)/shard_map/pallas_call | solution.py:408
  301.8 0.0 copy-start.1
  301.8 0.0 copy-start
  301.8 2.3 copy.8
  304.1 0.0 copy-done.1
  304.1 0.6 copy.9
  304.7 0.0 copy-done
  304.7 0.6 copy.10
Async XLA Ops:
  301.8 2.3 copy-start.1
  301.8 2.9 copy-start

commit v2 on v1

--- a/solution.py
+++ b/solution.py
@@ -18,10 +18,10 @@
     nr, nc, noise, lat,
     out, row_out, col_out,
     noise_all, lat_all, logits, plan, rowb, mt, st, mc, sc, colp,
-    row_box, col_box, x_send, x_recv, own, z_low, z_high, num,
+    row_box, col_box, x_send, x_recv, own, z_low, z_high, num, turned, result, out_box, row_swap, col_swap,
     local_sem, ng_send, ng_recv, lg_send, lg_recv,
     row_send, row_recv, col_send, col_recv,
-    xs_sem, xr_sem, up_sem, low_sem, down_sem, high_sem,
+    xs_sem, xr_sem, up_sem, low_sem, down_sem, high_sem, swap_send, swap_recv, out_send, out_recv,
 ):
     rows, kn = noise.shape
     cols, kl = lat.shape
@@ -29,40 +29,56 @@
     hi = nc // 2
     groups = cols // LANES
     scale = 2.0 / (width * EPSILON)
-    r = lax.axis_index("row")
-    c = lax.axis_index("col")
-    h, l = lax.div(c, 2), lax.rem(c, 2)
-    rh, rl = lax.div(r, 2), lax.rem(r, 2)
+    row = lax.axis_index("row")
+    col = lax.axis_index("col")
+    ch, cl = lax.div(col, 2), lax.rem(col, 2)
+    rh, rl = lax.div(row, 2), lax.rem(row, 2)
+    r, c = 2 * rh + cl, 2 * ch + rl
+    h, l = ch, rl
+    turn = rl != cl
+    half_r = nr // 2
+
+    def along_col(j):
+        return {"row": 2 * rh + lax.rem(j, 2), "col": 2 * lax.div(j, 2) + cl}
+
+    def along_row(j):
+        return {"row": 2 * lax.div(j, 2) + rl, "col": 2 * ch + lax.rem(j, 2)}
+
+    across = {"row": 2 * rh + 1 - rl, "col": 2 * ch + 1 - cl}
 
     barrier = pltpu.get_barrier_semaphore()
+
+    def greet(device):
+        pl.semaphore_signal(barrier, inc=1, device_id=device, device_id_type=MESH)
+
     for d in range(1, nc):
-        pl.semaphore_signal(barrier, inc=1, device_id={"col": lax.rem(c + d, nc)}, device_id_type=MESH)
+        greet(along_col(lax.rem(c + d, nc)))
     for d in range(1, nr):
-        pl.semaphore_signal(barrier, inc=1, device_id={"row": lax.rem(r + d, nr)}, device_id_type=MESH)
-    pl.semaphore_wait(barrier, nc - 1 + nr - 1)
+        greet(along_row(lax.rem(r + d, nr)))
+    for d in range(1, half_r):
+        greet({"row": 2 * lax.rem(rh + d, half_r) + 1 - rl, "col": col})
+    greet(across)
+    pl.semaphore_wait(barrier, nc - 1 + nr - 1 + half_r - 1 + 1)
 
     def noise_slot(j):
         return noise_all.at[lax.div(j, 2), :, pl.ds(pl.multiple_of(lax.rem(j, 2) * kn, kn), kn)]
 
-    def lat_slot(j):
-        return lat_all.at[j]
-
-    def remote(src, dst, send, recv, axis, target):
+    def remote(src, dst, send, recv, device):
         return pltpu.make_async_remote_copy(
             src_ref=src, dst_ref=dst, send_sem=send, recv_sem=recv,
-            device_id={axis: target}, device_id_type=MESH,
+            device_id=device, device_id_type=MESH,
         )
 
     class Gather:
-        def __init__(self, axis, n, own_ref, slot, send, recv, ah, al):
-            self.axis, self.half, self.own, self.slot = axis, n // 2, own_ref, slot
+        def __init__(self, along, n, own_ref, slot, send, recv, ah, al):
+            self.along, self.half, self.own, self.slot = along, n // 2, own_ref, slot
             self.send, self.recv, self.h, self.l = send, recv, ah, al
             self.me = 2 * ah + al
 
         def copy(self, kind, j, src):
             target = (self.me + 1 - 2 * self.l, self.me + 2, self.me - 2)[kind]
             return remote(
-                src, self.slot(j), self.send.at[kind, lax.div(j, 2)], self.recv.at[j], self.axis, target
+                src, self.slot(j), self.send.at[kind, lax.div(j, 2)], self.recv.at[j], self.along(target)
             )
 
         def first(self):
@@ -119,16 +135,147 @@
                 def _():
                     self.copy(2, j, self.slot(j)).wait_send()
 
-    noise_g = Gather("col", nc, noise, noise_slot, ng_send, ng_recv, h, l)
-    lat_g = Gather("row", nr, lat, lat_slot, lg_send, lg_recv, rh, rl)
-    noise_g.first()
-    lat_g.first()
-    mine = [
-        pltpu.make_async_copy(noise, noise_slot(c), local_sem.at[0]),
-        pltpu.make_async_copy(lat, lat_slot(r), local_sem.at[1]),
-    ]
-    for copy in mine:
-        copy.start()
+    noise_g = Gather(along_col, nc, noise, noise_slot, ng_send, ng_recv, h, l)
+    half = cols // 2
+
+    def lat_part(j, p):
+        return lat_all.at[j, pl.ds(p * half, half)]
+
+    def lat_own(p):
+        return lat.at[pl.ds(p * half, half)]
+
+    def lat_copy(kind, j, p, src=None):
+        home = {"row": 2 * rh + cl, "col": col}
+        side = {"row": 2 * rh + cl, "col": 2 * ch + 1 - cl}
+        up = {"row": 2 * (rh + 1) + cl, "col": col}
+        down = {"row": 2 * (rh - 1) + cl, "col": col}
+        device = (home, side, up, down)[kind]
+        return remote(
+            lat_part(j, p) if src is None else src, lat_part(j, p),
+            lg_send.at[kind, j, p], lg_recv.at[j, p], device,
+        )
+
+    def lat_relay(kind, j, p):
+        device = (
+            None, {"row": row, "col": 2 * ch + 1 - cl},
+            {"row": row + 2, "col": col}, {"row": row - 2, "col": col},
+        )[kind]
+        return remote(lat_part(j, p), lat_part(j, p), lg_send.at[kind, j, p], lg_recv.at[j, p], device)
+
+    def lat_arrived(j, p):
+        lat_relay(1, j, p).wait_recv()
+
+    def lat_ends(act):
+        for p in (1, 0):
+            act(lat_copy(1, row, p, lat_own(p)))
+
+            @pl.when(turn)
+            def _():
+                act(lat_copy(0, row, p, lat_own(p)))
+
+        for p in (0, 1):
+            @pl.when(rh < half_r - 1)
+            def _():
+                act(lat_copy(2, row, p, lat_own(p)))
+
+            @pl.when(rh > 0)
+            def _():
+                act(lat_copy(3, row, p, lat_own(p)))
+
+    def lat_pass(act, wait):
+        @pl.when(turn)
+        def _():
+            for q in range(2):
+                j = 2 * rh + q
+                wait(j, 1)
+
+                @pl.when(rh < half_r - 1)
+                def _():
+                    act(lat_relay(2, j, 1))
+
+                @pl.when(rh > 0)
+                def _():
+                    act(lat_relay(3, j, 1))
+
+        for s in range(1, half_r):
+            for sign, kind in ((-1, 2), (1, 3)):
+                k = rh + sign * s
+                onward = (rh < half_r - 1) if sign < 0 else (rh > 0)
+                valid = (k >= 0) if sign < 0 else (k < half_r)
+
+                @pl.when(valid)
+                def _():
+                    for q in range(2):
+                        j = 2 * k + q
+                        if half_r > 2:
+                            @pl.when(turn)
+                            def _():
+                                wait(j, 1)
+
+                                @pl.when(onward)
+                                def _():
+                                    act(lat_relay(kind, j, 1))
+
+                        @pl.when(jnp.logical_not(turn))
+                        def _():
+                            wait(j, 0)
+                            act(lat_relay(1, j, 0))
+
+                            @pl.when(onward)
+                            def _():
+                                act(lat_relay(kind, j, 0))
+                                wait(j, 1)
+                                act(lat_relay(kind, j, 1))
+
+    def lat_ready(k):
+        kh, kq = lax.div(k, 2), lax.rem(k, 2)
+        near = kh == rh
+        onward = ((kh < rh) & (rh < half_r - 1)) | ((kh > rh) & (rh > 0))
+
+        @pl.when(turn)
+        def _():
+            lat_arrived(k, 0)
+            if half_r == 2:
+                @pl.when(jnp.logical_not(near))
+                def _():
+                    lat_arrived(k, 1)
+
+        @pl.when(jnp.logical_not(turn) & near & (kq != rl))
+        def _():
+            lat_arrived(k, 0)
+            lat_arrived(k, 1)
+
+        @pl.when(jnp.logical_not(turn) & jnp.logical_not(near) & jnp.logical_not(onward))
+        def _():
+            lat_arrived(k, 1)
+
+    noise_swap = remote(noise, turned, swap_send.at[0], swap_recv.at[0], across)
+
+    @pl.when(turn)
+    def _():
+        noise_swap.start()
+
+    @pl.when(jnp.logical_not(turn))
+    def _():
+        noise_g.first()
+
+    lat_ends(lambda copy: copy.start())
+    keep_noise = pltpu.make_async_copy(noise, noise_slot(c), local_sem.at[0])
+    keep_turned = pltpu.make_async_copy(turned, noise_slot(c), local_sem.at[0])
+    keep_lat = pltpu.make_async_copy(lat, lat_all.at[row], local_sem.at[1])
+
+    @pl.when(jnp.logical_not(turn))
+    def _():
+        keep_noise.start()
+        keep_lat.start()
+
+    @pl.when(turn)
+    def _():
+        noise_swap.wait_recv()
+        noise_g.own = turned
+        noise_g.first()
+        keep_turned.start()
+
     colp[...] = jnp.zeros_like(colp)
 
     tile_n = min(256, cols)
@@ -146,47 +293,47 @@
             else:
                 logits[:, span] = part
 
-    def blocks(s):
-        @pl.loop(0, 2)
-        def _(side):
-            k = h + s * (2 * side - 1)
-
-            @pl.when((k >= 0) & (k < hi))
-            def _():
-                noise_g.other(k)
-                block(k, True)
-
-    for s in range(1, min(3, hi)):
+    def noise_ready(k):
+        noise_g.other(k)
+
+    noise_g.forward(1)
+    lat_pass(lambda copy: copy.start(), lat_arrived)
+    for s in range(2, hi - 1):
         noise_g.forward(s)
-    for s in range(1, nr // 2):
-        lat_g.forward(s)
-    for copy in mine:
-        copy.wait()
-
-    @pl.loop(0, nr // 2)
-    def _(k):
-        lat_g.other(k)
-
-    noise_g.other(h)
-    block(h, False)
-    if hi > 1:
-        blocks(1)
-    for s in range(3, hi):
-        noise_g.forward(s)
-        blocks(s - 1)
+
+    @pl.when(jnp.logical_not(turn))
+    def _():
+        keep_noise.wait()
+        keep_lat.wait()
+
+    @pl.when(turn)
+    def _():
+        keep_turned.wait()
+
+    near = jnp.minimum(jnp.maximum(h, 2 * rh), 2 * rh + 1)
+    noise_ready(near)
+    lat_ready(near)
+    block(near, False)
     if hi > 2:
-        blocks(hi - 1)
-
-    def exchange(axis, n, me, box, send, recv):
+        noise_g.forward(hi - 1)
+
+    @pl.loop(1, hi)
+    def _(i):
+        k = jnp.where(i == 1, 4 * rh + 1 - near, lax.rem(2 * rh + i, hi))
+        noise_ready(k)
+        lat_ready(k)
+        block(k, True)
+
+    def exchange(along, n, me, box, send, recv):
         for d in range(1, n):
-            remote(box.at[me], box.at[me], send.at[d], recv.at[me], axis, lax.rem(me + d, n)).start()
+            remote(box.at[me], box.at[me], send.at[d], recv.at[me], along(lax.rem(me + d, n))).start()
         for d in range(1, n):
             j = lax.rem(me + n - d, n)
-            remote(box.at[j], box.at[j], send.at[d], recv.at[j], axis, j).wait_recv()
-
-    def sent(axis, n, me, box, send, recv):
+            remote(box.at[j], box.at[j], send.at[d], recv.at[j], along(j)).wait_recv()
+
+    def sent(along, n, me, box, send, recv):
         for d in range(1, n):
-            remote(box.at[me], box.at[me], send.at[d], recv.at[me], axis, lax.rem(me + d, n)).wait_send()
+            remote(box.at[me], box.at[me], send.at[d], recv.at[me], along(lax.rem(me + d, n))).wait_send()
 
     def merged(n, box):
         high = functools.reduce(jnp.maximum, [box[j, 0:1, :] for j in range(n)])
@@ -216,9 +363,9 @@
         mine_box = box.at[c]
         mine_box[0:1, :] = high
         mine_box[1:2, :] = jnp.sum(st[...].T * jnp.exp(m - high), axis=0, keepdims=True)
-        exchange("col", nc, c, box, row_send.at[step], row_recv.at[step])
+        exchange(along_col, nc, c, box, row_send.at[step], row_recv.at[step])
         rowp = -math.log(rows * nr) - merged(nc, box)
-        row_out[...] = rowp
+        row_swap[0] = rowp
         rowb[...] = jnp.broadcast_to(rowp, (LANES, rows)).T
 
         @pl.loop(0, rows // col_tile)
@@ -238,9 +385,21 @@
         mine_box = box.at[r]
         mine_box[0:1, :] = high
         mine_box[1:2, :] = jnp.sum(sc[...] * jnp.exp(m - high), axis=0, keepdims=True)
-        exchange("row", nr, r, box, col_send.at[step], col_recv.at[step])
+        exchange(along_row, nr, r, box, col_send.at[step], col_recv.at[step])
         colp[...] = -math.log(cols * nc) - merged(nr, box)
-    col_out[...] = colp[...]
+    row_pair = remote(row_swap.at[0], row_swap.at[1], swap_send.at[1], swap_recv.at[1], across)
+    col_pair = remote(colp, col_swap, swap_send.at[2], swap_recv.at[2], across)
+
+    @pl.when(turn)
+    def _():
+        row_pair.start()
+        col_pair.start()
+
+    @pl.when(jnp.logical_not(turn))
+    def _():
+        row_out[...] = row_swap[0]
+        col_out[...] = colp[...]
+
 
     @pl.loop(0, rows // row_tile, unroll=2)
     def _(t):
@@ -264,16 +423,25 @@
                 plan[...], lat_all[k, :, pl.ds(src, tile_k)], preferred_element_type=jnp.float32
             ).astype(jnp.bfloat16)
 
-    partner = c + 1 - 2 * l
+    parts = 2
+    part = rows // parts
+    add_tile = min(128, part)
+
+    def piece(ref, k, p):
+        return ref.at[k, pl.ds(p * part, part)]
 
     def x_copy(k):
-        return remote(x_send.at[k], x_recv.at[k], xs_sem.at[k], xr_sem.at[k], "col", partner)
-
-    def up_copy(k):
-        return remote(own.at[k], z_low.at[k], up_sem.at[k], low_sem.at[k], "col", c + 2)
-
-    def down_copy(k):
-        return remote(own.at[k], z_high.at[k], down_sem.at[k], high_sem.at[k], "col", c - 2)
+        return remote(x_send.at[k], x_recv.at[k], xs_sem.at[k], xr_sem.at[k], along_col(c + 1 - 2 * l))
+
+    def up_copy(k, p):
+        return remote(
+            piece(own, k, p), piece(z_low, k, p), up_sem.at[k, p], low_sem.at[k, p], along_col(c + 2)
+        )
+
+    def down_copy(k, p):
+        return remote(
+            piece(own, k, p), piece(z_high, k, p), down_sem.at[k, p], high_sem.at[k, p], along_col(c - 2)
+        )
 
     def farthest_first(body):
         @pl.loop(0, 2 * hi - 1)
@@ -289,114 +457,140 @@
         share(k, 1 - l, x_send.at[k])
         x_copy(k).start()
 
-    farthest_first(send_share)
+    f32, bf16 = jnp.float32, jnp.bfloat16
+
+    def tiles(p, body):
+        @pl.loop(0, part // add_tile)
+        def _(t):
+            body(pl.ds(pl.multiple_of(p * part + t * add_tile, add_tile), add_tile))
+
+    def add(k, p, third):
+        def body(span):
+            total = own[k, span, :].astype(f32) + third[k, span, :].astype(f32)
+            own[k, span, :] = total.astype(bf16)
+        tiles(p, body)
+
+    def first_relay(k):
+        x_copy(k).wait_recv()
+        for p in range(parts):
+            add(k, p, x_recv)
+
+            @pl.when((k > h) & (h == 0))
+            def _():
+                up_copy(k, p).start()
+
+            @pl.when((k < h) & (h == hi - 1))
+            def _():
+                down_copy(k, p).start()
+
+    def work(k):
+        send_share(k)
+        share(k, l, own.at[k])
+        first_relay(k)
+
+    farthest_first(work)
 
     mine_box = row_box.at[ITERS, c]
     mine_box[0:1, :] = jnp.sum(mt[...].T, axis=0, keepdims=True)
-    mine_box[1:2, :] = jnp.zeros((1, rows), jnp.float32)
-    exchange("col", nc, c, row_box.at[ITERS], row_send.at[ITERS], row_recv.at[ITERS])
+    mine_box[1:2, :] = jnp.zeros((1, rows), f32)
+    exchange(along_col, nc, c, row_box.at[ITERS], row_send.at[ITERS], row_recv.at[ITERS])
     mass = functools.reduce(jnp.add, [row_box[ITERS, j, 0:1, :] for j in range(nc)])
     rowb[...] = jnp.broadcast_to(1.0 / mass, (LANES, rows)).T
 
-    farthest_first(lambda k: share(k, l, own.at[k]))
-
-    f32 = jnp.float32
-    add_tile = min(128, rows)
-
-    def tiles(body):
-        @pl.loop(0, rows // add_tile)
-        def _(t):
-            body(pl.ds(pl.multiple_of(t * add_tile, add_tile), add_tile))
-
-    def add_two(k):
-        def body(span):
-            own[k, span, :] = (own[k, span, :].astype(f32) + x_recv[k, span, :].astype(f32)).astype(jnp.bfloat16)
-        tiles(body)
-
-    def add_three(k, third):
-        def body(span):
-            own[k, span, :] = (
-                own[k, span, :].astype(f32) + x_recv[k, span, :].astype(f32) + third[k, span, :].astype(f32)
-            ).astype(jnp.bfloat16)
-        tiles(body)
-
     def relay(k):
-        x_copy(k).wait_recv()
-
-        @pl.when(k > h)
-        def _():
-            @pl.when(h > 0)
-            def _():
-                up_copy(k).wait_recv()
-                add_three(k, z_low)
-
-            @pl.when(h == 0)
-            def _():
-                add_two(k)
-
-            up_copy(k).start()
-
-        @pl.when(k < h)
-        def _():
-            @pl.when(h < hi - 1)
-            def _():
-                down_copy(k).wait_recv()
-                add_three(k, z_high)
-
-            @pl.when(h == hi - 1)
-            def _():
-                add_two(k)
-
-            down_copy(k).start()
+        for p in range(parts):
+            @pl.when((k > h) & (h > 0))
+            def _():
+                up_copy(k, p).wait_recv()
+                add(k, p, z_low)
+                up_copy(k, p).start()
+
+            @pl.when((k < h) & (h < hi - 1))
+            def _():
+                down_copy(k, p).wait_recv()
+                add(k, p, z_high)
+                down_copy(k, p).start()
 
     farthest_first(relay)
 
-    def start_sum(span):
-        num[span, :] = own[h, span, :].astype(f32) + x_recv[h, span, :].astype(f32)
-
-    tiles(start_sum)
-
-    @pl.when(h > 0)
-    def _():
-        up_copy(h).wait_recv()
-
-        def body(span):
+    def out_copy(p):
+        span = pl.ds(p * part, part)
+        return remote(result.at[span], out_box.at[span], out_send.at[p], out_recv.at[p], across)
+
+    for p in range(parts):
+        def start_sum(span):
+            num[span, :] = own[h, span, :].astype(f32)
+
+        tiles(p, start_sum)
+
+        def add_low(span):
             num[span, :] += z_low[h, span, :].astype(f32)
-        tiles(body)
-
-    @pl.when(h < hi - 1)
-    def _():
-        down_copy(h).wait_recv()
-
-        def body(span):
+
+        def add_high(span):
             num[span, :] += z_high[h, span, :].astype(f32)
-        tiles(body)
-
-    def last(span):
-        inverse = rowb[span, :]
-        for g in range(kn // LANES):
-            out[span, lane(g)] = (num[span, lane(g)] * inverse).astype(jnp.bfloat16)
-
-    tiles(last)
+
+        @pl.when(h > 0)
+        def _():
+            up_copy(h, p).wait_recv()
+            tiles(p, add_low)
+
+        @pl.when(h < hi - 1)
+        def _():
+            down_copy(h, p).wait_recv()
+            tiles(p, add_high)
+
+        def divide(ref):
+            def body(span):
+                inverse = rowb[span, :]
+                for g in range(kn // LANES):
+                    ref[span, lane(g)] = (num[span, lane(g)] * inverse).astype(bf16)
+            tiles(p, body)
+
+        @pl.when(turn)
+        def _():
+            divide(result)
+            out_copy(p).start()
+
+        @pl.when(jnp.logical_not(turn))
+        def _():
+            divide(out)
+
+    @pl.when(turn)
+    def _():
+        row_pair.wait()
+        col_pair.wait()
+        row_out[...] = row_swap[1]
+        col_out[...] = col_swap[...]
+        for p in range(parts):
+            out_copy(p).wait_recv()
+
+            def body(span):
+                out[span, :] = out_box[span, :]
+            tiles(p, body)
+        for p in range(parts):
+            out_copy(p).wait_send()
+        noise_swap.wait_send()
 
     noise_g.finish()
-    lat_g.finish()
+    lat_ends(lambda copy: copy.wait_send())
+    lat_pass(lambda copy: copy.wait_send(), lambda j, p: None)
     for step in range(ITERS + 1):
-        sent("col", nc, c, row_box.at[step], row_send.at[step], row_recv.at[step])
+        sent(along_col, nc, c, row_box.at[step], row_send.at[step], row_recv.at[step])
     for step in range(ITERS):
-        sent("row", nr, r, col_box.at[step], col_send.at[step], col_recv.at[step])
+        sent(along_row, nr, r, col_box.at[step], col_send.at[step], col_recv.at[step])
 
     @pl.loop(0, hi)
     def _(k):
         x_copy(k).wait_send()
 
-        @pl.when(k > h)
-        def _():
-            up_copy(k).wait_send()
-
-        @pl.when(k < h)
-        def _():
-            down_copy(k).wait_send()
+        for p in range(parts):
+            @pl.when(k > h)
+            def _():
+                up_copy(k, p).wait_send()
+
+            @pl.when(k < h)
+            def _():
+                down_copy(k, p).wait_send()
 
 
 def on_device(nr, nc, noise, latents):
@@ -433,12 +627,18 @@
             vmem((hi, rows, kn), bf16),
             vmem((hi, rows, kn), bf16),
             vmem((rows, kn), f32),
+            vmem((rows, kn), bf16),
+            vmem((rows, kn), bf16),
+            vmem((rows, kn), bf16),
+            vmem((2, 1, rows), f32),
+            vmem((1, cols), f32),
             dma((2,)),
             dma((3, hi)), dma((nc,)),
-            dma((3, nr // 2)), dma((nr,)),
+            dma((4, nr, 2)), dma((nr, 2)),
             dma((ITERS + 1, nc)), dma((ITERS + 1, nc)),
             dma((ITERS, nr)), dma((ITERS, nr)),
-            dma((hi,)), dma((hi,)), dma((hi,)), dma((hi,)), dma((hi,)), dma((hi,)),
+            dma((hi,)), dma((hi,)), dma((hi, 2)), dma((hi, 2)), dma((hi, 2)), dma((hi, 2)),
+            dma((3,)), dma((3,)), dma((2,)), dma((2,)),
         ],
         compiler_params=pltpu.CompilerParams(
             collective_id=0, has_side_effects=True, vmem_limit_bytes=58 * 2**20

time: 310 us -> 258 us (0.83); the launches traced: 305 us -> 257 us
  Pallas kernels: 301 us -> 253 us
    pallas_call x1, Pallas kernels: 301 us -> 253 us  [on_device(): pl.pallas_call(functools.partial(kernel, nr, nc), out_shape=(jax.ShapeDty...]
where the time goes in v2:
time: 258 us; the launch traced here: 257 us
  Pallas kernels  253 us (98%)
  local copies, waits for them, and re-layouts  3.46 us (1%)
    pallas_call x1, Pallas kernels, on_device(): pl.pallas_call(functools.partial(kernel, nr, nc), out_shape=(jax.ShapeDty...  253 us

profile of v2, /device:TPU:9, one launch (start us, length us, event | category | flops | bytes accessed | tf_op | source)
XLA Modules:
  0.0 257.4 jit_solution(13281578126539404673)
XLA Ops:
  0.6 253.3 %shard_map.49 = (bf16[1024,512]{1,0:T(8,128)(2,1)}, f32[1,1024]{1,0:T(1,128)}, f32[1,1024]{1,0:T(1,128)}) custom-call(bf16[1024,512]{1,0:T(8,128)(2,1)} %noise.1, bf16[1024,1024]{1,0:T(8,128)(2,1)} %lat.1), custom_call_target="tpu_custom_call" | custom-call | flops 17179869184 | bytes 8388608 | tf_op jit(solution)/shard_map/pallas_call | solution.py:602
  253.9 0.0 copy-start.1
  253.9 0.0 copy-start
  253.9 2.3 copy.8
  256.2 0.0 copy-done.1
  256.2 0.6 copy.9
  256.8 0.0 copy-done
  256.8 0.6 copy.10
Async XLA Ops:
  253.9 2.3 copy-start.1
  253.9 2.9 %copy-start = (f32[1,1024]{1,0:T(1,128)S(1)}, f32[1,1024]{1,0:T(1,128)}, u32[]{:S(2)}) copy-start(f32[1,1024]{1,0:T(1,128)} %get-tuple-element.8) | copy-start | bytes 12292

commit v3 on v2

--- a/solution.py
+++ b/solution.py
@@ -136,13 +136,14 @@
                     self.copy(2, j, self.slot(j)).wait_send()
 
     noise_g = Gather(along_col, nc, noise, noise_slot, ng_send, ng_recv, h, l)
-    half = cols // 2
+    cut = cols * 3 // 8
+    lat_span = (pl.ds(0, cut), pl.ds(cut, cols - cut))
 
     def lat_part(j, p):
-        return lat_all.at[j, pl.ds(p * half, half)]
+        return lat_all.at[j, lat_span[p]]
 
     def lat_own(p):
-        return lat.at[pl.ds(p * half, half)]
+        return lat.at[lat_span[p]]
 
     def lat_copy(kind, j, p, src=None):
         home = {"row": 2 * rh + cl, "col": col}
@@ -165,22 +166,28 @@
     def lat_arrived(j, p):
         lat_relay(1, j, p).wait_recv()
 
-    def lat_ends(act):
+    def lat_side(act):
         for p in (1, 0):
             act(lat_copy(1, row, p, lat_own(p)))
 
-            @pl.when(turn)
-            def _():
-                act(lat_copy(0, row, p, lat_own(p)))
-
-        for p in (0, 1):
-            @pl.when(rh < half_r - 1)
-            def _():
-                act(lat_copy(2, row, p, lat_own(p)))
-
-            @pl.when(rh > 0)
-            def _():
-                act(lat_copy(3, row, p, lat_own(p)))
+    def lat_home(act):
+        for p in (1, 0):
+            act(lat_copy(0, row, p, lat_own(p)))
+
+    def lat_line(act, p):
+        @pl.when(rh < half_r - 1)
+        def _():
+            act(lat_copy(2, row, p, lat_own(p)))
+
+        @pl.when(rh > 0)
+        def _():
+            act(lat_copy(3, row, p, lat_own(p)))
+
+    def start(copy):
+        copy.start()
+
+    def wait_send(copy):
+        copy.wait_send()
 
     def lat_pass(act, wait):
         @pl.when(turn)
@@ -259,7 +266,7 @@
     def _():
         noise_g.first()
 
-    lat_ends(lambda copy: copy.start())
+    lat_line(start, 0)
     keep_noise = pltpu.make_async_copy(noise, noise_slot(c), local_sem.at[0])
     keep_turned = pltpu.make_async_copy(turned, noise_slot(c), local_sem.at[0])
     keep_lat = pltpu.make_async_copy(lat, lat_all.at[row], local_sem.at[1])
@@ -274,7 +281,9 @@
         noise_swap.wait_recv()
         noise_g.own = turned
         noise_g.first()
+        lat_side(start)
         keep_turned.start()
+        lat_home(start)
 
     colp[...] = jnp.zeros_like(colp)
 
@@ -297,7 +306,14 @@
         noise_g.other(k)
 
     noise_g.forward(1)
-    lat_pass(lambda copy: copy.start(), lat_arrived)
+
+    @pl.when(jnp.logical_not(turn))
+    def _():
+        lat_side(start)
+
+    lat_line(wait_send, 0)
+    lat_line(start, 1)
+    lat_pass(start, lat_arrived)
     for s in range(2, hi - 1):
         noise_g.forward(s)
 
@@ -414,24 +430,30 @@
 
     tile_k = min(256, kn)
 
-    def share(k, side, dst):
+    parts = 4
+    part = rows // parts
+    add_tile = min(128, part)
+
+    def rows_of(p):
+        return pl.ds(pl.multiple_of(p * part, part), part)
+
+    def share(k, side, p, dst):
         @pl.loop(0, kn // tile_k)
         def _(t):
             off = pl.multiple_of(t * tile_k, tile_k)
             src = pl.multiple_of(side * kn + t * tile_k, tile_k)
-            dst[:, pl.ds(off, tile_k)] = jnp.dot(
-                plan[...], lat_all[k, :, pl.ds(src, tile_k)], preferred_element_type=jnp.float32
+            dst[k, rows_of(p), pl.ds(off, tile_k)] = jnp.dot(
+                plan[rows_of(p), :], lat_all[k, :, pl.ds(src, tile_k)], preferred_element_type=jnp.float32
             ).astype(jnp.bfloat16)
 
-    parts = 2
-    part = rows // parts
-    add_tile = min(128, part)
-
     def piece(ref, k, p):
-        return ref.at[k, pl.ds(p * part, part)]
-
-    def x_copy(k):
-        return remote(x_send.at[k], x_recv.at[k], xs_sem.at[k], xr_sem.at[k], along_col(c + 1 - 2 * l))
+        return ref.at[k, rows_of(p)]
+
+    def x_copy(k, p):
+        return remote(
+            piece(x_send, k, p), piece(x_recv, k, p), xs_sem.at[k, p], xr_sem.at[k, p],
+            along_col(c + 1 - 2 * l),
+        )
 
     def up_copy(k, p):
         return remote(
@@ -453,10 +475,6 @@
             def _():
                 body(k)
 
-    def send_share(k):
-        share(k, 1 - l, x_send.at[k])
-        x_copy(k).start()
-
     f32, bf16 = jnp.float32, jnp.bfloat16
 
     def tiles(p, body):
@@ -470,9 +488,16 @@
             own[k, span, :] = total.astype(bf16)
         tiles(p, body)
 
-    def first_relay(k):
-        x_copy(k).wait_recv()
-        for p in range(parts):
+    def work(k):
+        @pl.loop(0, parts)
+        def _(p):
+            share(k, 1 - l, p, x_send)
+            x_copy(k, p).start()
+
+        @pl.loop(0, parts)
+        def _(p):
+            share(k, l, p, own)
+            x_copy(k, p).wait_recv()
             add(k, p, x_recv)
 
             @pl.when((k > h) & (h == 0))
@@ -482,11 +507,6 @@
             @pl.when((k < h) & (h == hi - 1))
             def _():
                 down_copy(k, p).start()
-
-    def work(k):
-        send_share(k)
-        share(k, l, own.at[k])
-        first_relay(k)
 
     farthest_first(work)
 
@@ -498,7 +518,8 @@
     rowb[...] = jnp.broadcast_to(1.0 / mass, (LANES, rows)).T
 
     def relay(k):
-        for p in range(parts):
+        @pl.loop(0, parts)
+        def _(p):
             @pl.when((k > h) & (h > 0))
             def _():
                 up_copy(k, p).wait_recv()
@@ -514,10 +535,11 @@
     farthest_first(relay)
 
     def out_copy(p):
-        span = pl.ds(p * part, part)
+        span = rows_of(p)
         return remote(result.at[span], out_box.at[span], out_send.at[p], out_recv.at[p], across)
 
-    for p in range(parts):
+    @pl.loop(0, parts)
+    def _(p):
         def start_sum(span):
             num[span, :] = own[h, span, :].astype(f32)
 
@@ -572,8 +594,14 @@
         noise_swap.wait_send()
 
     noise_g.finish()
-    lat_ends(lambda copy: copy.wait_send())
-    lat_pass(lambda copy: copy.wait_send(), lambda j, p: None)
+    lat_side(wait_send)
+    lat_line(wait_send, 1)
+
+    @pl.when(turn)
+    def _():
+        lat_home(wait_send)
+
+    lat_pass(wait_send, lambda j, p: None)
     for step in range(ITERS + 1):
         sent(along_col, nc, c, row_box.at[step], row_send.at[step], row_recv.at[step])
     for step in range(ITERS):
@@ -581,9 +609,10 @@
 
     @pl.loop(0, hi)
     def _(k):
-        x_copy(k).wait_send()
-
-        for p in range(parts):
+        @pl.loop(0, parts)
+        def _(p):
+            x_copy(k, p).wait_send()
+
             @pl.when(k > h)
             def _():
                 up_copy(k, p).wait_send()
@@ -637,8 +666,8 @@
             dma((4, nr, 2)), dma((nr, 2)),
             dma((ITERS + 1, nc)), dma((ITERS + 1, nc)),
             dma((ITERS, nr)), dma((ITERS, nr)),
-            dma((hi,)), dma((hi,)), dma((hi, 2)), dma((hi, 2)), dma((hi, 2)), dma((hi, 2)),
-            dma((3,)), dma((3,)), dma((2,)), dma((2,)),
+            dma((hi, 4)), dma((hi, 4)), dma((hi, 4)), dma((hi, 4)), dma((hi, 4)), dma((hi, 4)),
+            dma((3,)), dma((3,)), dma((4,)), dma((4,)),
         ],
         compiler_params=pltpu.CompilerParams(
             collective_id=0, has_side_effects=True, vmem_limit_bytes=58 * 2**20

time: 258 us -> 254 us (0.984)
  Pallas kernels: 253 us -> 250 us
    pallas_call x1, Pallas kernels: 253 us -> 250 us  [on_device(): pl.pallas_call(functools.partial(kernel, nr, nc), out_shape=(jax.ShapeDty...]
where the time goes in v3:
time: 254 us
  Pallas kernels  250 us (98%)
  local copies, waits for them, and re-layouts  3.46 us (1%)
    pallas_call x1, Pallas kernels, on_device(): pl.pallas_call(functools.partial(kernel, nr, nc), out_shape=(jax.ShapeDty...  250 us

profile of v3, /device:TPU:9, one launch (start us, length us, event | category | flops | bytes accessed | tf_op | source)
XLA Modules:
  0.0 254.3 jit_solution(12365907603045925835)
XLA Ops:
  0.6 250.2 %shard_map.49 = (bf16[1024,512]{1,0:T(8,128)(2,1)}, f32[1,1024]{1,0:T(1,128)}, f32[1,1024]{1,0:T(1,128)}) custom-call(bf16[1024,512]{1,0:T(8,128)(2,1)} %noise.1, bf16[1024,1024]{1,0:T(8,128)(2,1)} %lat.1), custom_call_target="tpu_custom_call" | custom-call | flops 17179869184 | bytes 8388608 | tf_op jit(solution)/shard_map/pallas_call | solution.py:631
  250.8 0.0 copy-start.1
  250.8 0.0 copy-start
  250.8 2.3 copy.8
  253.1 0.0 copy-done.1
  253.1 0.6 copy.9
  253.7 0.0 copy-done
  253.7 0.6 copy.10
Async XLA Ops:
  250.8 2.3 copy-start.1
  250.8 2.9 %copy-start = (f32[1,1024]{1,0:T(1,128)S(1)}, f32[1,1024]{1,0:T(1,128)}, u32[]{:S(2)}) copy-start(f32[1,1024]{1,0:T(1,128)} %get-tuple-element.8) | copy-start | bytes 12292

commit v4 on v3

--- a/solution.py
+++ b/solution.py
@@ -267,6 +267,7 @@
         noise_g.first()
 
     lat_line(start, 0)
+    lat_line(start, 1)
     keep_noise = pltpu.make_async_copy(noise, noise_slot(c), local_sem.at[0])
     keep_turned = pltpu.make_async_copy(turned, noise_slot(c), local_sem.at[0])
     keep_lat = pltpu.make_async_copy(lat, lat_all.at[row], local_sem.at[1])
@@ -311,11 +312,9 @@
     def _():
         lat_side(start)
 
-    lat_line(wait_send, 0)
-    lat_line(start, 1)
-    lat_pass(start, lat_arrived)
     for s in range(2, hi - 1):
         noise_g.forward(s)
+    lat_pass(start, lat_arrived)
 
     @pl.when(jnp.logical_not(turn))
     def _():
@@ -595,6 +594,7 @@
 
     noise_g.finish()
     lat_side(wait_send)
+    lat_line(wait_send, 0)
     lat_line(wait_send, 1)
 
     @pl.when(turn)

time: 254 us -> 264 us (1.039)
  Pallas kernels: 250 us -> 260 us
    pallas_call x1, Pallas kernels: 250 us -> 260 us  [on_device(): pl.pallas_call(functools.partial(kernel, nr, nc), out_shape=(jax.ShapeDty...]
where the time goes in v4:
time: 264 us
  Pallas kernels  260 us (98%)
  local copies, waits for them, and re-layouts  3.46 us (1%)
    pallas_call x1, Pallas kernels, on_device(): pl.pallas_call(functools.partial(kernel, nr, nc), out_shape=(jax.ShapeDty...  260 us

profile of v4, /device:TPU:9, one launch (start us, length us, event | category | flops | bytes accessed | tf_op | source)
XLA Modules:
  0.0 264.3 jit_solution(1401601692101261181)
XLA Ops:
  0.6 260.1 %shard_map.49 = (bf16[1024,512]{1,0:T(8,128)(2,1)}, f32[1,1024]{1,0:T(1,128)}, f32[1,1024]{1,0:T(1,128)}) custom-call(bf16[1024,512]{1,0:T(8,128)(2,1)} %noise.1, bf16[1024,1024]{1,0:T(8,128)(2,1)} %lat.1), custom_call_target="tpu_custom_call" | custom-call | flops 17179869184 | bytes 8388608 | tf_op jit(solution)/shard_map/pallas_call | solution.py:631
  260.8 0.0 copy-start.1
  260.8 0.0 copy-start
  260.8 2.3 copy.8
  263.1 0.0 copy-done.1
  263.1 0.6 copy.9
  263.7 0.0 copy-done
  263.7 0.6 copy.10
Async XLA Ops:
  260.8 2.3 copy-start.1
  260.8 2.9 %copy-start = (f32[1,1024]{1,0:T(1,128)S(1)}, f32[1,1024]{1,0:T(1,128)}, u32[]{:S(2)}) copy-start(f32[1,1024]{1,0:T(1,128)} %get-tuple-element.8) | copy-start | bytes 12292

commit v5 on v3

--- a/solution.py
+++ b/solution.py
@@ -166,9 +166,8 @@
     def lat_arrived(j, p):
         lat_relay(1, j, p).wait_recv()
 
-    def lat_side(act):
-        for p in (1, 0):
-            act(lat_copy(1, row, p, lat_own(p)))
+    def lat_side(act, p):
+        act(lat_copy(1, row, p, lat_own(p)))
 
     def lat_home(act):
         for p in (1, 0):
@@ -281,7 +280,7 @@
         noise_swap.wait_recv()
         noise_g.own = turned
         noise_g.first()
-        lat_side(start)
+        lat_side(start, 1)
         keep_turned.start()
         lat_home(start)
 
@@ -309,11 +308,12 @@
 
     @pl.when(jnp.logical_not(turn))
     def _():
-        lat_side(start)
+        lat_side(start, 1)
 
     lat_line(wait_send, 0)
     lat_line(start, 1)
     lat_pass(start, lat_arrived)
+    lat_side(start, 0)
     for s in range(2, hi - 1):
         noise_g.forward(s)
 
@@ -594,7 +594,8 @@
         noise_swap.wait_send()
 
     noise_g.finish()
-    lat_side(wait_send)
+    lat_side(wait_send, 0)
+    lat_side(wait_send, 1)
     lat_line(wait_send, 1)
 
     @pl.when(turn)

time: 254 us -> 261 us (1.028)
  Pallas kernels: 250 us -> 257 us
    pallas_call x1, Pallas kernels: 250 us -> 257 us  [on_device(): pl.pallas_call(functools.partial(kernel, nr, nc), out_shape=(jax.ShapeDty...]
where the time goes in v5:
time: 261 us
  Pallas kernels  257 us (98%)
  local copies, waits for them, and re-layouts  3.46 us (1%)
    pallas_call x1, Pallas kernels, on_device(): pl.pallas_call(functools.partial(kernel, nr, nc), out_shape=(jax.ShapeDty...  257 us

profile of v5, /device:TPU:9, one launch (start us, length us, event | category | flops | bytes accessed | tf_op | source)
XLA Modules:
  0.0 260.9 jit_solution(8299239731224391916)
XLA Ops:
  0.6 256.8 %shard_map.49 = (bf16[1024,512]{1,0:T(8,128)(2,1)}, f32[1,1024]{1,0:T(1,128)}, f32[1,1024]{1,0:T(1,128)}) custom-call(bf16[1024,512]{1,0:T(8,128)(2,1)} %noise.1, bf16[1024,1024]{1,0:T(8,128)(2,1)} %lat.1), custom_call_target="tpu_custom_call" | custom-call | flops 17179869184 | bytes 8388608 | tf_op jit(solution)/shard_map/pallas_call | solution.py:632
  257.4 0.0 copy-start.1
  257.4 0.0 copy-start
  257.4 2.3 copy.8
  259.7 0.0 copy-done.1
  259.7 0.6 copy.9
  260.3 0.0 copy-done
  260.3 0.6 copy.10
Async XLA Ops:
  257.4 2.3 copy-start.1
  257.4 2.9 %copy-start = (f32[1,1024]{1,0:T(1,128)S(1)}, f32[1,1024]{1,0:T(1,128)}, u32[]{:S(2)}) copy-start(f32[1,1024]{1,0:T(1,128)} %get-tuple-element.8) | copy-start | bytes 12292

commit v6 on v4

--- a/solution.py
+++ b/solution.py
@@ -266,8 +266,14 @@
     def _():
         noise_g.first()
 
+    lat_side(start)
     lat_line(start, 0)
     lat_line(start, 1)
+
+    @pl.when(turn)
+    def _():
+        lat_home(start)
+
     keep_noise = pltpu.make_async_copy(noise, noise_slot(c), local_sem.at[0])
     keep_turned = pltpu.make_async_copy(turned, noise_slot(c), local_sem.at[0])
     keep_lat = pltpu.make_async_copy(lat, lat_all.at[row], local_sem.at[1])
@@ -282,9 +288,7 @@
         noise_swap.wait_recv()
         noise_g.own = turned
         noise_g.first()
-        lat_side(start)
         keep_turned.start()
-        lat_home(start)
 
     colp[...] = jnp.zeros_like(colp)
 
@@ -308,13 +312,9 @@
 
     noise_g.forward(1)
 
-    @pl.when(jnp.logical_not(turn))
-    def _():
-        lat_side(start)
-
+    lat_pass(start, lat_arrived)
     for s in range(2, hi - 1):
         noise_g.forward(s)
-    lat_pass(start, lat_arrived)
 
     @pl.when(jnp.logical_not(turn))
     def _():

time: 264 us -> 255 us (0.966)
  Pallas kernels: 260 us -> 250 us
    pallas_call x1, Pallas kernels: 260 us -> 250 us  [on_device(): pl.pallas_call(functools.partial(kernel, nr, nc), out_shape=(jax.ShapeDty...]
where the time goes in v6:
time: 255 us
  Pallas kernels  250 us (98%)
  local copies, waits for them, and re-layouts  3.46 us (1%)
    pallas_call x1, Pallas kernels, on_device(): pl.pallas_call(functools.partial(kernel, nr, nc), out_shape=(jax.ShapeDty...  250 us

profile of v6, /device:TPU:9, one launch (start us, length us, event | category | flops | bytes accessed | tf_op | source)
XLA Modules:
  0.0 254.6 jit_solution(28168558450642867)
XLA Ops:
  0.6 250.5 %shard_map.49 = (bf16[1024,512]{1,0:T(8,128)(2,1)}, f32[1,1024]{1,0:T(1,128)}, f32[1,1024]{1,0:T(1,128)}) custom-call(bf16[1024,512]{1,0:T(8,128)(2,1)} %noise.1, bf16[1024,1024]{1,0:T(8,128)(2,1)} %lat.1), custom_call_target="tpu_custom_call" | custom-call | flops 17179869184 | bytes 8388608 | tf_op jit(solution)/shard_map/pallas_call | solution.py:631
  251.1 0.0 copy-start.1
  251.1 0.0 copy-start
  251.1 2.3 copy.8
  253.4 0.0 copy-done.1
  253.4 0.6 copy.9
  254.0 0.0 copy-done
  254.0 0.6 copy.10
Async XLA Ops:
  251.1 2.3 copy-start.1
  251.1 2.9 %copy-start = (f32[1,1024]{1,0:T(1,128)S(1)}, f32[1,1024]{1,0:T(1,128)}, u32[]{:S(2)}) copy-start(f32[1,1024]{1,0:T(1,128)} %get-tuple-element.8) | copy-start | bytes 12292
